TPU v7x, 256 devices: a whole 4x4x8 slice. The times are simulated.
256 devices in a mesh: grp: 8 (over y, x_lo), pen: 32 (over x_hi, z, core).
Axes of the slice: x: 4 (x_hi: 2, x_lo: 2; x = x_hi * 2 + x_lo), y: 4, z: 8, core: 2. Of those that a mesh axis runs over, the one named last changes fastest.
Arguments:
- field: float32 [8, 64, 64, 64, 128], P('grp', 'pen'), may hold values from -6 to 6
- upstream: bfloat16 [8, 64, 64, 64, 128], P('grp', 'pen'), may hold values from -6 to 6
- mode_weights: bfloat16 [16, 32, 16, 2, 128, 128], P(None, 'pen', 'grp'), may hold values from -1.5 to 1.5
- skip_weight: float32 [128, 128], replicated, may hold values from -0.5 to 0.5
- channel_bias: float32 [128], replicated, may hold values from -3 to 3
Outputs:
- output: bfloat16 [8, 64, 64, 64, 128], P('grp', 'pen')
- weight_grad: bfloat16 [16, 32, 16, 2, 128, 128], P(None, 'pen', 'grp')
All inputs are finite; a program needn't handle non-finite values.
Results may differ from a plain program's by a relative error of at most 0.006.
Values may be sent and summed in bfloat16 or wider, within the bound.
A program may use at most 64 MiB of HBM per device.

v0:
```python
import math

import jax
import jax.numpy as jnp
from jax import lax
from jax.sharding import PartitionSpec as P

NX = 64
NY = 64
NZ = 64
MX = 16
MY = 32
MZ = 16


highest = lax.Precision.HIGHEST


def freq_table(length, number, signed):
    mode_index = jnp.arange(number, dtype=jnp.int32)
    if signed:
        frequency = jnp.where(mode_index < number // 2, mode_index, mode_index - number)
    else:
        frequency = mode_index
    cell_index = jnp.arange(length, dtype=jnp.int32)
    phase_turns = cell_index[:, None] * frequency[None, :] % length
    angles = phase_turns.astype(jnp.float32) * (2.0 * math.pi / length)
    return (jnp.cos(angles), jnp.sin(angles))


def complex_table(length, number, direction):
    cosine, sine = freq_table(length, number, True)
    norming = 1.0 / math.sqrt(length)
    real_row = jnp.stack([cosine, direction * sine], axis=-1)
    imag_row = jnp.stack([-direction * sine, cosine], axis=-1)
    return jnp.stack([real_row, imag_row], axis=-2) * norming


def paired(spectrum):
    real_part = spectrum[..., 0:1, :]
    imag_part = spectrum[..., 1:2, :]
    real_row = jnp.concatenate([real_part, -imag_part], axis=-2)
    imag_row = jnp.concatenate([imag_part, real_part], axis=-2)
    return jnp.stack([real_row, imag_row], axis=-3)


def exact_gelu(values):
    return jax.nn.gelu(values, approximate=False)


def send_modes(values):
    return lax.all_to_all(values, "grp", split_axis=3, concat_axis=0, tiled=True)


def send_pencil(values):
    return lax.all_to_all(values, "pen", split_axis=2, concat_axis=1, tiled=True)


def return_pencil(values):
    return lax.all_to_all(values, "pen", split_axis=1, concat_axis=2, tiled=True)


def return_owner(values):
    return lax.all_to_all(values, "grp", split_axis=0, concat_axis=3, tiled=True)


def first_forward(values, plane_table):
    return jnp.einsum("bxyzqc,xkqp->bkyzpc", values, plane_table, precision=highest)


def first_inverse(values, plane_back):
    return jnp.einsum("bkyzqc,kxqp->bxyzpc", values, plane_back, precision=highest)


def to_modes(values, depth_table, row_table, plane_table):
    planes = jnp.einsum("bxyzc,zkp->bxykpc", values, depth_table, precision=highest)
    planes = jnp.einsum("bxykqc,yjqp->bxjkpc", planes, row_table, precision=highest)
    planes = first_forward(send_pencil(planes), plane_table)
    return send_modes(planes.astype(jnp.bfloat16))


def from_modes(modes, depth_back, row_back, plane_back):
    planes = return_pencil(first_inverse(return_owner(modes), plane_back))
    planes = jnp.einsum("bxjkqc,jyqp->bxykpc", planes, row_back, precision=highest)
    return jnp.einsum("bxykqc,kqz->bxyzc", planes, depth_back, precision=highest)


def shards(field, upstream, mode_weights, skip_weight, channel_bias):
    depth_cos, depth_sin = freq_table(NZ, MZ, False)
    depth_norm = 1.0 / math.sqrt(NZ)
    depth_weight = jnp.where(jnp.arange(MZ) == 0, 1.0, 2.0).astype(jnp.float32)
    depth_forward = jnp.stack([depth_cos, -depth_sin], axis=-1) * depth_norm
    depth_cotangent = depth_forward * depth_weight[None, :, None]
    depth_back = jnp.stack([depth_cos.T, -depth_sin.T], axis=1) * (
        depth_weight[:, None, None] * depth_norm
    )
    row_forward = complex_table(NY, MY, -1.0)
    row_back = jnp.transpose(complex_table(NY, MY, 1.0), (1, 0, 2, 3))
    plane_forward = complex_table(NX, MX, -1.0)
    plane_back = jnp.transpose(complex_table(NX, MX, 1.0), (1, 0, 2, 3))
    spectrum = to_modes(field, depth_forward, row_forward, plane_forward)
    paired_spec = paired(spectrum)
    mixed_modes = jnp.einsum(
        "bxyzpqi,xyzqio->bxyzpo", paired_spec, mode_weights, preferred_element_type=jnp.float32
    )
    spectral = from_modes(mixed_modes, depth_back, row_back, plane_back)
    skip_part = jnp.dot(field, skip_weight, precision=highest)
    pre_act = spectral + skip_part + channel_bias
    output = exact_gelu(pre_act).astype(jnp.bfloat16)
    _, pullback = jax.vjp(exact_gelu, pre_act)
    pre_grad = pullback(upstream.astype(jnp.float32))[0]
    mode_grad = to_modes(pre_grad, depth_cotangent, row_forward, plane_forward)
    weight_grad = jnp.einsum(
        "bxyzpqi,bxyzpo->xyzqio", paired_spec, mode_grad, preferred_element_type=jnp.float32
    )
    return (output, weight_grad.astype(jnp.bfloat16))


def solution(mesh):
    in_specs = (
        P("grp", "pen", None, None, None),
        P("grp", "pen", None, None, None),
        P(None, "pen", "grp", None, None, None),
        P(),
        P(),
    )
    out_specs = (P("grp", "pen", None, None, None), P(None, "pen", "grp", None, None, None))
    return jax.shard_map(shards, mesh=mesh, in_specs=in_specs, out_specs=out_specs, check_vma=False)
```

profile of v0, /device:TPU:1, one launch (start us, length us, event | category | flops | bytes accessed | tf_op | source)
XLA Modules:
  0.0 181.1 jit_solution(7038274935766350024)
XLA Ops:
  0.9 0.6 fusion.72
  1.5 3.9 %fusion.35 = f32[2,64,16,2,128]{4,2,1,0,3:T(8,128)S(1)} fusion(f32[1,2,64,64,128]{4,3,2,1,0:T(8,128)} %param.5, f32[64,16,1]{0,1,2:T(8,128)S(1)} %get-tuple-element.36, f32[64,16,1]{0,1,2:T(8,128)S(1)} %get-tuple-element.37), kind=kOutput, calls=%fused_computation.47 | convolution fusion | flops 402657280 | bytes 6299648 | tf_op jit(solution)/shard_map/bxyzc,zkp->bxykpc/dot_general | solution.py:76
  5.4 1.9 %fusion.42 = f32[1,2,32,16,2,128]{5,2,3,1,4,0:T(8,128)S(1)} fusion(f32[2,64,16,2,128]{4,2,1,0,3:T(8,128)S(1)} %fusion.35, f32[64,32,1,2]{0,1,3,2:T(8,128)S(1)} %get-tuple-element.18, f32[64,32,1,2]{0,1,3,2:T(8,128)S(1)} %get-tuple-element.21), kind=kOutput, calls=%fused_computation.51 | convolution fusion | flops 402669568 | bytes 3178496 | tf_op jit(solution)/shard_map/bxykqc,yjqp->bxjkpc/dot_general | solution.py:77
  7.3 1.6 copy.65
  8.9 12.6 %all-to-all-start = ((f32[1,2,32,16,2,128]{5,3,1,4,0,2:T(8,128)}), f32[1,2,32,16,2,128]{5,3,1,4,0,2:T(8,128)S(1)}, u32[]{:S(2)}, u32[]{:S(2)}) async-start(f32[1,2,32,16,2,128]{5,3,1,4,0,2:T(8,128)} %copy.65), calls=%async_computation | async-start | bytes 2097152 | tf_op jit(solution)/shard_map/all_to_all | solution.py:56
  21.6 0.6 fusion.84
  22.2 27.0 %all-to-all-done = f32[1,2,32,16,2,128]{5,3,1,4,0,2:T(8,128)S(1)} async-done(((f32[1,2,32,16,2,128]{5,3,1,4,0,2:T(8,128)}), f32[1,2,32,16,2,128]{5,3,1,4,0,2:T(8,128)S(1)}, u32[]{:S(2)}, u32[]{:S(2)}) %all-to-all-start) | async-done | bytes 1048608 | tf_op jit(solution)/shard_map/all_to_all | solution.py:56
  49.3 1.2 fusion.54
  50.6 9.6 %all_to_all.93 = bf16[1,16,1,16,2,128]{5,1,4,2,0,3:T(8,128)(2,1)S(1)} all-to-all(bf16[1,16,1,16,2,128]{5,1,4,2,0,3:T(8,128)(2,1)S(1)} %copy.69), channel_id=1, replica_groups=mesh['grp'=8,'pen'=32] {'grp'}, dimensions={3} | all-to-all | bytes 262144 | tf_op jit(solution)/shard_map/all_to_all | solution.py:52
  60.8 8.5 %all_to_all.94 = f32[8,16,1,2,2,128]{5,4,3,1,2,0:T(2,128)S(1)} all-to-all(f32[8,16,1,2,2,128]{5,4,3,1,2,0:T(2,128)S(1)} %copy.72), channel_id=1, replica_groups=mesh['grp'=8,'pen'=32] {'grp'}, dimensions={0} | all-to-all | bytes 524288 | tf_op jit(solution)/shard_map/all_to_all | solution.py:64
  69.4 1.0 convolution_bitcast_fusion.1
  70.5 1.6 copy.75
  72.0 9.4 %all-to-all-start.3 = ((f32[1,64,1,16,2,128]{5,3,4,2,0,1:T(8,128)}), f32[1,64,1,16,2,128]{5,3,4,2,0,1:T(8,128)S(1)}, u32[]{:S(2)}, u32[]{:S(2)}) async-start(f32[1,64,1,16,2,128]{5,3,4,2,0,1:T(8,128)} %copy.75), calls=%async_computation.3 | async-start | bytes 2097152 | tf_op jit(solution)/shard_map/all_to_all | solution.py:60
  82.1 6.5 %fusion.14 = f32[2,64,64,128]{3,2,1,0:T(8,128)} fusion(f32[1,2,64,64,128]{4,3,2,1,0:T(8,128)} %param.5, f32[128,128]{1,0:T(8,128)} %param.8), kind=kOutput, calls=%fused_computation.17 | convolution fusion | flops 1610612736 | bytes 8454144 | tf_op jit(solution)/shard_map/dot_general | solution.py:107
  88.6 20.5 %all-to-all-done.3 = f32[1,64,1,16,2,128]{5,3,4,2,0,1:T(8,128)S(1)} async-done(((f32[1,64,1,16,2,128]{5,3,4,2,0,1:T(8,128)}), f32[1,64,1,16,2,128]{5,3,4,2,0,1:T(8,128)S(1)}, u32[]{:S(2)}, u32[]{:S(2)}) %all-to-all-start.3) | async-done | bytes 1048608 | tf_op jit(solution)/shard_map/all_to_all | solution.py:60
  109.1 3.1 %convolution_bitcast_fusion = f32[2,64,16,2,128]{4,1,2,0,3:T(8,128)S(1)} fusion(f32[1,32,2,1,16,2,128]{6,4,5,3,2,1,0:T(8,128)S(1)} %bitcast.247, f32[64,32,1,2]{0,1,2,3:T(8,128)} %get-tuple-element.22, f32[64,32,1,2]{0,1,2,3:T(8,128)S(1)} %get-tuple-element.17), kind=kOutput, calls=%fused_computation.49 | convolution fusion | flops 402669568 | bytes 3178496 | tf_op jit(solution)/shard_map/bxjkqc,jyqp->bxykpc/dot_general | solution.py:84
  112.3 17.2 %multiply_convert_fusion = (bf16[1,2,64,64,128]{4,3,2,1,0:T(8,128)(2,1)}, f32[1,2,64,64,128]{4,3,2,1,0:T(8,128)S(1)}, f32[1,2,64,64,128]{4,3,2,1,0:T(8,128)S(1)}) fusion(f32[128]{0:T(128)} %param.9, f32[2,64,64,128]{3,2,1,0:T(8,128)} %fusion.14, f32[2,64,16,2,128]{4,1,2,0,3:T(8,128)S(1)} %convolution_bitcast_fusion, ...), kind=kOutput, calls=%fused_computation.19 | convolution fusion | flops 472911872 | bytes 16785984 | tf_op jit(solution)/shard_map/bxykqc,kqz->bxyzc/dot_general | solution.py:85
  129.5 4.0 %fusion.38 = f32[2,64,16,2,128]{4,2,1,0,3:T(8,128)S(1)} fusion(bf16[1,2,64,64,128]{4,3,2,1,0:T(8,128)(2,1)S(1)} %copy-done.6, f32[1,2,64,64,128]{4,3,2,1,0:T(8,128)S(1)} %get-tuple-element.11, f32[1,2,64,64,128]{4,3,2,1,0:T(8,128)S(1)} %get-tuple-element.35, f32[64,16,1]{0,1,2:T(8,128)S(1)} %copy-done.3, f32[64,16,1]{0,1,2:T(8,128)S(1)} %copy-done.5, ...), kind=kOutput, calls=%fused_computation.48 | convolution fusion | flops 417337344 | bytes 12591168 | tf_op jit(solution)/shard_map/bxyzc,zkp->bxykpc/dot_general | solution.py:76
  133.5 1.9 %fusion.45 = f32[1,2,32,16,2,128]{5,2,3,1,4,0:T(8,128)S(1)} fusion(f32[2,64,16,2,128]{4,2,1,0,3:T(8,128)S(1)} %fusion.38, f32[64,32,1,2]{0,1,3,2:T(8,128)S(1)} %get-tuple-element.18, f32[64,32,1,2]{0,1,3,2:T(8,128)S(1)} %get-tuple-element.21), kind=kOutput, calls=%fused_computation.52 | convolution fusion | flops 402669568 | bytes 3178496 | tf_op jit(solution)/shard_map/bxykqc,yjqp->bxjkpc/dot_general | solution.py:77
  135.4 0.6 copy.79
  136.0 33.8 %all_to_all.95 = f32[1,2,32,16,2,128]{5,3,1,4,0,2:T(8,128)S(1)} all-to-all(f32[1,2,32,16,2,128]{5,3,1,4,0,2:T(8,128)S(1)} %copy.79), channel_id=1, replica_groups=mesh['grp'=8,'pen'=32] {'pen'}, dimensions={2} | all-to-all | bytes 2097152 | tf_op jit(solution)/shard_map/all_to_all | solution.py:56
  169.9 1.2 fusion.53
  171.1 7.9 %all_to_all.96 = bf16[1,16,1,16,2,128]{5,1,4,2,0,3:T(8,128)(2,1)S(1)} all-to-all(bf16[1,16,1,16,2,128]{5,1,4,2,0,3:T(8,128)(2,1)S(1)} %copy.83), channel_id=1, replica_groups=mesh['grp'=8,'pen'=32] {'grp'}, dimensions={3} | all-to-all | bytes 262144 | tf_op jit(solution)/shard_map/all_to_all | solution.py:52
  179.1 2.1 %fusion.41 = bf16[16,1,2,2,128,128]{5,4,3,2,1,0:T(8,128)(2,1)} fusion(bf16[8,16,1,2,1,2,128]{6,0,5,4,3,1,2:T(8,128)(2,1)S(1)} %get-tuple-element.16, bf16[8,16,1,2,1,2,128]{6,0,5,4,3,1,2:T(8,128)(2,1)S(1)} %get-tuple-element.15, bf16[8,16,2,2,128,1]{4,1,3,2,0,5:T(8,128)(2,1)S(1)} %bitcast.251), kind=kOutput, calls=%fused_computation.50 | convolution fusion | flops 34734080 | bytes 2490368 | tf_op jit(solution)/shard_map/bxyzpqi,bxyzpo->xyzqio/dot_general | solution.py:113
  (33 shorter events, 2.0 us)
Async XLA Ops:
  0.6 59.7 %copy-start = (bf16[16,1,2,2,128,128]{5,4,3,2,1,0:T(8,128)(2,1)S(1)}, bf16[16,1,2,2,128,128]{5,4,3,2,1,0:T(8,128)(2,1)}, u32[]{:S(2)}) copy-start(bf16[16,1,2,2,128,128]{5,4,3,2,1,0:T(8,128)(2,1)} %param.7) | copy-start | bytes 6291460
  0.7 6.5 %copy-start.2 = (f32[64,16,1]{0,1,2:T(8,128)}, f32[64,16,1]{0,1,2:T(8,128)S(1)}, u32[]{:S(2)}) copy-start(f32[64,16,1]{0,1,2:T(8,128)S(1)} %get-tuple-element.36) | copy-start | bytes 12292
  0.7 6.5 %copy-start.4 = (f32[64,16,1]{0,1,2:T(8,128)}, f32[64,16,1]{0,1,2:T(8,128)S(1)}, u32[]{:S(2)}) copy-start(f32[64,16,1]{0,1,2:T(8,128)S(1)} %get-tuple-element.37) | copy-start | bytes 12292
  8.9 40.3 %all-to-all-start = ((f32[1,2,32,16,2,128]{5,3,1,4,0,2:T(8,128)}), f32[1,2,32,16,2,128]{5,3,1,4,0,2:T(8,128)S(1)}, u32[]{:S(2)}, u32[]{:S(2)}) async-start(f32[1,2,32,16,2,128]{5,3,1,4,0,2:T(8,128)} %copy.65), calls=%async_computation | async-start | bytes 2097152 | tf_op jit(solution)/shard_map/all_to_all | solution.py:56
  49.2 20.2 %copy-start.1 = (f32[64,16,1,2]{0,1,3,2:T(8,128)S(1)}, f32[64,16,1,2]{0,1,3,2:T(8,128)}, u32[]{:S(2)}) copy-start(f32[64,16,1,2]{0,1,3,2:T(8,128)} %get-tuple-element.28) | copy-start | bytes 24580
  72.0 37.1 %all-to-all-start.3 = ((f32[1,64,1,16,2,128]{5,3,4,2,0,1:T(8,128)}), f32[1,64,1,16,2,128]{5,3,4,2,0,1:T(8,128)S(1)}, u32[]{:S(2)}, u32[]{:S(2)}) async-start(f32[1,64,1,16,2,128]{5,3,4,2,0,1:T(8,128)} %copy.75), calls=%async_computation.3 | async-start | bytes 2097152 | tf_op jit(solution)/shard_map/all_to_all | solution.py:60
  112.2 17.3 %copy-start.3 = (f32[64,16,1]{0,1,2:T(8,128)S(1)}, f32[64,16,1]{0,1,2:T(8,128)}, u32[]{:S(2)}) copy-start(f32[64,16,1]{0,1,2:T(8,128)} %copy-done.2) | copy-start | bytes 12292
  112.2 17.3 %copy-start.5 = (f32[64,16,1]{0,1,2:T(8,128)S(1)}, f32[64,16,1]{0,1,2:T(8,128)}, u32[]{:S(2)}) copy-start(f32[64,16,1]{0,1,2:T(8,128)} %copy-done.4) | copy-start | bytes 12292
  112.3 17.3 %copy-start.6 = (bf16[1,2,64,64,128]{4,3,2,1,0:T(8,128)(2,1)S(1)}, bf16[1,2,64,64,128]{4,3,2,1,0:T(8,128)(2,1)}, u32[]{:S(2)}) copy-start(bf16[1,2,64,64,128]{4,3,2,1,0:T(8,128)(2,1)} %param.6) | copy-start | bytes 6291460
  112.3 17.3 %copy-start.7 = (f32[16]{0:T(128)S(1)}, f32[16]{0:T(128)}, u32[]{:S(2)}) copy-start(f32[16]{0:T(128)} %fusion.127) | copy-start | bytes 196
where the time goes:
time: 184 us; the launch traced here: 181 us
  blocking collectives  59.8 us (32%)
  waiting for transfers between devices  47.5 us (26%)
  matrix products  44.3 us (24%)
  starting transfers between devices  21.9 us (12%)
  local copies, waits for them, and re-layouts  4.32 us (2%)
  other arithmetic  2.31 us (1%)
    all_to_all x1, blocking collectives, send_pencil(): lax.all_to_all(values, 'pen', split_axis=2, concat_axis=1, tiled=True)  33.8 us
    all_to_all x1, waiting for transfers between devices, send_pencil(): lax.all_to_all(values, 'pen', split_axis=2, concat_axis=1, tiled=True)  27 us
    all_to_all x1, waiting for transfers between devices, return_pencil(): lax.all_to_all(values, 'pen', split_axis=1, concat_axis=2, tiled=True)  20.5 us
    all_to_all x2, blocking collectives, send_modes(): lax.all_to_all(values, 'grp', split_axis=3, concat_axis=0, tiled=True)  17.5 us
    dot_general x1, matrix products, from_modes(): jnp.einsum('bxykqc,kqz->bxyzc', planes, depth_back, precision=highest)  17.2 us
    all_to_all x1, starting transfers between devices, send_pencil(): lax.all_to_all(values, 'pen', split_axis=2, concat_axis=1, tiled=True)  12.6 us
    all_to_all x1, starting transfers between devices, return_pencil(): lax.all_to_all(values, 'pen', split_axis=1, concat_axis=2, tiled=True)  9.35 us
    all_to_all x1, blocking collectives, return_owner(): lax.all_to_all(values, 'grp', split_axis=0, concat_axis=3, tiled=True)  8.55 us
  transfers between devices with their start and end apart: 2, of which 2 were waited for; matrix products, arithmetic and copies ran while one was open for 4% of the time, Pallas kernels for 0%

commit v1 on v0

v1 whole, which is shorter than its diff:
```python
import functools
import math

import jax
import jax.numpy as jnp
import ml_dtypes
import numpy as np
from jax import lax
from jax.experimental import pallas as pl
from jax.experimental.pallas import tpu as pltpu
from jax.sharding import PartitionSpec as P

MESH = pl.DeviceIdType.MESH
f32 = jnp.float32
bf16 = jnp.bfloat16


def rotation(angle, inverse):
    cosine, sine = np.cos(angle), np.sin(angle)
    sign = -1.0 if inverse else 1.0
    real_row = np.stack([cosine, sign * sine], axis=-1)
    imag_row = np.stack([-sign * sine, cosine], axis=-1)
    return np.stack([real_row, imag_row], axis=-2) / 8.0


def halves(table, axis):
    high = table.astype(ml_dtypes.bfloat16)
    low = (table - high.astype(np.float64)).astype(ml_dtypes.bfloat16)
    return np.concatenate([high, low], axis=axis)


def make_tables():
    turn = 2.0 * math.pi / 64.0
    cell = np.arange(64)
    depth = turn * (np.arange(16)[:, None] * cell[None, :] % 64)
    weight = np.where(np.arange(16) == 0, 1.0, 2.0)[:, None, None]
    depth = np.stack([np.cos(depth), -np.sin(depth)], axis=1) / 8.0
    by_parity = lambda t: t.reshape(8, 2, 2, 64).transpose(1, 0, 2, 3)
    eye = np.eye
    t1 = np.einsum("carz,yw->cayrwz", by_parity(depth), eye(4)).reshape(128, 256)
    t6 = np.einsum("carz,yw->yzcawr", by_parity(depth * weight), eye(4)).reshape(256, 128)
    ky = np.arange(16)[None, :] - 16 * np.arange(2)[:, None]
    row = turn * (ky[:, :, None] * cell % 64)
    t2 = np.einsum("hdyrs,ab->dahrbys", rotation(row, False), eye(2)).reshape(128, 256)
    t5 = np.einsum("hdyrs,ab->ayrdbhs", rotation(row, True), eye(4)).reshape(512, 256)
    kx = np.where(np.arange(16) < 8, np.arange(16), np.arange(16) - 16)
    plane = turn * (kx[:, None] * cell % 64)
    forward = rotation(plane, False).reshape(16, 2, 16, 2, 2, 2)
    backward = rotation(plane, True).reshape(16, 2, 16, 2, 2, 2)
    t3 = np.einsum("kXserv,ab,hi->Xeahkrsbiv", forward, eye(4), eye(2)).reshape(2, 2, 256, 256)
    t4 = np.einsum("kXserv,ab,hi->Xesahribkv", backward, eye(4), eye(2)).reshape(2, 2, 256, 256)
    swap = np.eye(256).reshape(8, 32, 256).transpose(1, 0, 2).reshape(256, 256)
    return (
        halves(t1, 0),
        halves(t2, 0),
        halves(t3, 2),
        halves(t4, 2),
        halves(t5, 0),
        halves(t6, 1),
        np.concatenate([swap, swap], axis=1).astype(ml_dtypes.bfloat16),
        np.ascontiguousarray(swap.T).astype(ml_dtypes.bfloat16),
    )


def dot(left, right):
    return jnp.dot(left, right, preferred_element_type=f32)


def split(values):
    high = values.astype(bf16)
    return high, (values - high.astype(f32)).astype(bf16)


def dot_split(table, values):
    rows = table.shape[0] // 2
    both = dot(table, jnp.concatenate(split(values), axis=1))
    return both[:rows, :128] + both[:rows, 128:] + both[rows:, :128]


def dot_exact(table, values):
    rows = table.shape[0] // 2
    both = dot(table, values)
    return both[:rows] + both[rows:]


SCALED = (
    0.11283793162135076,
    0.11283476245314182,
    0.10392192770562217,
    0.0842669599289443,
    0.07073040277585074,
    -0.002833797179664962,
    0.08457735964663142,
    -0.09147177273287684,
    0.025136288482206462,
)


def gelu_pair(v):
    bell = jnp.exp(-0.5 * (v * v))
    t = 1.0 / (1.0 + 0.282842712474619 * jnp.abs(v))
    series = jnp.full_like(t, SCALED[-1] * 1.0)
    for coefficient in SCALED[-2::-1]:
        series = series * t + coefficient
    tail = bell * (t * series)
    phi = jnp.where(v >= 0, 1.0 - tail, tail)
    return v * phi, phi + v * (bell * (1.0 / math.sqrt(2.0 * math.pi)))


def kernel(
    field_hbm, up_hbm, weight_hbm, skip_hbm, bias_hbm, t1_hbm, t2_hbm, t3_hbm, t4_hbm, t5_hbm, t6_hbm, gather_hbm, scatter_hbm,
    out_hbm, grad_hbm,
    field, up, weight, skip, bias, t1, t2, t3, t4, t5, t6, gather, scatter,
    base, out, grad, zbuf, ybuf, rows, pairs, mixed,
    ring_send, ring_recv, wide_send, wide_recv, back_send, back_recv,
    load_sem, ring_ssem, ring_rsem, wide_ssem, wide_rsem, back_ssem, back_rsem, store_sem,
):
    g = lax.axis_index("grp")
    p = lax.axis_index("pen")
    x_hi = p // 16
    d = lax.rem(p, 16)
    w = g * 2 + x_hi

    def ring_peer(i):
        to = lax.rem(d + i, 16)
        return to, (g, x_hi * 16 + to)

    def wide_peer(i):
        to = lax.rem(w + i, 16)
        return to, (to // 2, lax.rem(to, 2) * 16 + d)

    barrier = pltpu.get_barrier_semaphore()

    def greet(i, carry):
        for peer in (ring_peer, wide_peer):
            pl.semaphore_signal(barrier, inc=1, device_id=peer(i)[1], device_id_type=MESH)
        return carry

    lax.fori_loop(1, 16, greet, 0)

    loads = []

    def load(source, target):
        copy = pltpu.make_async_copy(source, target, load_sem.at[len(loads)])
        copy.start()
        loads.append(copy)
        return copy

    t1_load = load(t1_hbm, t1)
    quarters = [
        load(field_hbm.at[:, pl.ds(n * 1024, 1024), :], field.at[:, pl.ds(n * 1024, 1024), :]) for n in range(4)
    ]
    t2_load = load(t2_hbm, t2)
    skip_load = load(skip_hbm, skip)
    bias_load = load(bias_hbm, bias)
    t3_load = load(t3_hbm.at[x_hi], t3)
    gather_load = load(gather_hbm, gather)
    weight_load = load(weight_hbm, weight)
    scatter_load = load(scatter_hbm, scatter)
    t4_load = load(t4_hbm.at[x_hi], t4)
    t5_load = load(t5_hbm, t5)
    t6_load = load(t6_hbm, t6)
    up_load = load(up_hbm, up)

    def ring_start(n, e, c):
        source, target = ring_send.at[n, e, c], ring_recv.at[n, e, c]
        pltpu.make_async_copy(source.at[d], target.at[d], ring_rsem.at[n, e, c]).start()

        def send(i, carry):
            to, device = ring_peer(i)
            pltpu.make_async_remote_copy(
                src_ref=source.at[to],
                dst_ref=target.at[d],
                send_sem=ring_ssem.at[n, e, c],
                recv_sem=ring_rsem.at[n, e, c],
                device_id=device,
                device_id_type=MESH,
            ).start()
            return carry

        lax.fori_loop(1, 16, send, 0)

    def wide_start(n, c):
        source, target = wide_send.at[n, c], wide_recv.at[n, c]
        slot = x_hi * 8 + g
        pltpu.make_async_copy(source.at[w], target.at[slot], wide_rsem.at[n, c]).start()

        def send(i, carry):
            to, device = wide_peer(i)
            pltpu.make_async_remote_copy(
                src_ref=source.at[to],
                dst_ref=target.at[slot],
                send_sem=wide_ssem.at[n, c],
                recv_sem=wide_rsem.at[n, c],
                device_id=device,
                device_id_type=MESH,
            ).start()
            return carry

        lax.fori_loop(1, 16, send, 0)

    def back_start(c):
        source, target = back_send.at[c], back_recv.at[c]
        slot = (g // 4) * 8 + x_hi * 4 + lax.rem(g, 4)
        pltpu.make_async_copy(source.at[g], target.at[slot], back_rsem.at[c]).start()

        def send(i, carry):
            to, device = wide_peer(i)
            pltpu.make_async_remote_copy(
                src_ref=source.at[to // 2],
                dst_ref=target.at[slot],
                send_sem=back_ssem.at[c],
                recv_sem=back_rsem.at[c],
                device_id=device,
                device_id_type=MESH,
            ).start()
            return carry

        lax.fori_loop(1, 16, send, 0)

    def drain(buffer, semaphore):
        pltpu.make_async_copy(buffer, buffer, semaphore).wait()

    def depth_step(e, m, values):
        tile = dot_split(t1[...], values).reshape(16, 8, 128)
        zbuf[e, :, pl.ds(pl.multiple_of(m * 8, 8), 8), :] = tile

    def row_step(n, e, c):
        for q in range(2):
            tiles = []
            for half in range(2):
                first = c * 8 + q * 4 + half * 2
                values = zbuf[e, first : first + 2].reshape(256, 128)
                tiles.append(dot_split(t2[...], values).reshape(16, 8, 128))
            ring_send[n, e, c, :, q] = jnp.concatenate(tiles, axis=1).astype(bf16)

    def plane_step(n, c):
        for q in range(2):
            total = dot_exact(t3[0], ring_recv[n, 0, c, :, q].reshape(256, 128))
            total += dot_exact(t3[1], ring_recv[n, 1, c, :, q].reshape(256, 128))
            wide_send[n // 2, c, q * 8 : q * 8 + 8] = total.reshape(8, 32, 128)

    def collect(n, c):
        summed = (wide_recv[n, c, 0:8] + wide_recv[n, c, 8:16]).reshape(256, 128)
        rows[...] = dot(gather[...], jnp.concatenate(split(summed), axis=0))

    t1_load.wait()
    for n in range(4):
        quarters[n].wait()

        def depth_loop(m, carry):
            for e in range(2):
                values = field[e, pl.ds(pl.multiple_of(m * 256, 256), 256), :]
                depth_step(e, m, values)
            return carry

        lax.fori_loop(n * 4, n * 4 + 4, depth_loop, 0)
    t2_load.wait()
    for c in range(2):
        for e in range(2):
            row_step(0, e, c)
            if c == 0 and e == 0:
                pl.semaphore_wait(barrier, 30)
            ring_start(0, e, c)

    skip_load.wait()
    bias_load.wait()
    skip_row = jnp.concatenate(split(skip[...]), axis=1)
    skip_both = jnp.concatenate([skip_row, skip_row], axis=0)

    def skip_loop(m, carry):
        for e in range(2):
            here = pl.ds(pl.multiple_of(m * 256, 256), 256)
            both = dot(jnp.concatenate(split(field[e, here, :]), axis=1), skip_both)
            base[e, here, :] = both[:, :128] + both[:, 128:] + bias[...]
        return carry

    lax.fori_loop(0, 16, skip_loop, 0)

    t3_load.wait()
    for c in range(2):
        for e in range(2):
            drain(ring_recv.at[0, e, c], ring_rsem.at[0, e, c])
        plane_step(0, c)
        wide_start(0, c)

    gather_load.wait()
    weight_load.wait()
    scatter_load.wait()
    for c in range(2):
        drain(wide_recv.at[0, c], wide_rsem.at[0, c])
        collect(0, c)

        def mix_loop(m, carry):
            for i in range(4):
                k = m * 4 + i
                real = rows[pl.ds(pl.multiple_of(k * 16, 16), 8), :]
                imag = rows[pl.ds(pl.multiple_of(k * 16 + 8, 8), 8), :]
                upper = jnp.concatenate([real, -imag], axis=1)
                lower = jnp.concatenate([imag, real], axis=1)
                paired = jnp.concatenate([upper, lower], axis=0).astype(bf16)
                pairs[c, k] = paired
                mixed[pl.ds(pl.multiple_of(k * 16, 16), 16), :] = dot(paired, weight[k, c]).astype(bf16)
            return carry

        lax.fori_loop(0, 4, mix_loop, 0)
        back_send[c] = dot(scatter[...], mixed[...]).astype(bf16).reshape(8, 32, 128)
        back_start(c)

    t4_load.wait()
    for c in range(2):
        drain(back_recv.at[c], back_rsem.at[c])
        for q in range(2):
            values = back_recv[c, q * 8 : q * 8 + 8].reshape(256, 128)
            for e in range(2):
                ring_send[1, e, c, :, q] = dot_exact(t4[e], values).reshape(16, 16, 128).astype(bf16)
        ring_start(1, 0, c)
    ring_start(1, 1, 0)
    ring_start(1, 1, 1)

    t5_load.wait()
    t6_load.wait()
    up_load.wait()
    stores = []
    for e in range(2):
        for c in range(2):
            drain(ring_recv.at[1, e, c], ring_rsem.at[1, e, c])
            for q in range(2):
                first = c * 8 + q * 4
                values = ring_recv[1, e, c, :, q].reshape(256, 128)
                ybuf[first : first + 4] = dot_exact(t5[...], values).reshape(4, 128, 128)

        def cell_loop(m, carry):
            values = ybuf[:, pl.ds(pl.multiple_of(m * 8, 8), 8), :].reshape(128, 128)
            half = jnp.concatenate(split(values), axis=1)
            both = dot(t6[...], jnp.concatenate([half, half], axis=0))
            here = pl.ds(pl.multiple_of(m * 256, 256), 256)
            value, slope = gelu_pair(both[:, :128] + both[:, 128:] + base[e, here, :])
            out[e, here, :] = value.astype(bf16)
            depth_step(e, m, slope * up[e, here, :].astype(f32))
            return carry

        lax.fori_loop(0, 16, cell_loop, 0)
        store = pltpu.make_async_copy(out.at[e], out_hbm.at[e], store_sem.at[e])
        store.start()
        stores.append(store)
        for c in range(2):
            row_step(2, e, c)
            ring_start(2, e, c)

    for c in range(2):
        for e in range(2):
            drain(ring_recv.at[2, e, c], ring_rsem.at[2, e, c])
        plane_step(2, c)
        wide_start(1, c)

    for c in range(2):
        drain(wide_recv.at[1, c], wide_rsem.at[1, c])
        collect(1, c)
        scale = jnp.where(g == 0, 1.0, 2.0).astype(f32) if c == 0 else f32(2.0)

        def grad_loop(m, carry):
            for i in range(4):
                k = m * 4 + i
                cotangent = (rows[pl.ds(pl.multiple_of(k * 16, 16), 16), :] * scale).astype(bf16)
                product = lax.dot_general(
                    pairs[c, k], cotangent, (((0,), (0,)), ((), ())), preferred_element_type=f32
                )
                grad[c, k] = product.astype(bf16)
            return carry

        lax.fori_loop(0, 4, grad_loop, 0)
        store = pltpu.make_async_copy(grad.at[c], grad_hbm.at[:, c], store_sem.at[2 + c])
        store.start()
        stores.append(store)

    for n in range(3):
        for e in range(2):
            for c in range(2):
                drain(ring_send.at[n, e, c, pl.ds(0, 15)], ring_ssem.at[n, e, c])
    for n in range(2):
        for c in range(2):
            drain(wide_send.at[n, c, pl.ds(0, 15)], wide_ssem.at[n, c])
    for c in range(2):
        drain(back_recv.at[c, pl.ds(0, 15)], back_ssem.at[c])
    for store in stores:
        store.wait()


def shards(tables, field, upstream, mode_weights, skip_weight, channel_bias):
    anywhere = pl.BlockSpec(memory_space=pl.ANY)
    out, grad = pl.pallas_call(
        kernel,
        out_shape=(
            jax.ShapeDtypeStruct((2, 4096, 128), bf16),
            jax.ShapeDtypeStruct((16, 2, 256, 128), bf16),
        ),
        in_specs=[anywhere] * 13,
        out_specs=(anywhere, anywhere),
        scratch_shapes=[
            pltpu.VMEM((2, 4096, 128), f32),
            pltpu.VMEM((2, 4096, 128), bf16),
            pltpu.VMEM((16, 2, 256, 128), bf16),
            pltpu.VMEM((128, 128), f32),
            pltpu.VMEM((1, 128), f32),
            pltpu.VMEM((256, 256), bf16),
            pltpu.VMEM((256, 256), bf16),
            pltpu.VMEM((2, 512, 256), bf16),
            pltpu.VMEM((2, 512, 256), bf16),
            pltpu.VMEM((1024, 256), bf16),
            pltpu.VMEM((256, 256), bf16),
            pltpu.VMEM((256, 512), bf16),
            pltpu.VMEM((256, 256), bf16),
            pltpu.VMEM((2, 4096, 128), f32),
            pltpu.VMEM((2, 4096, 128), bf16),
            pltpu.VMEM((2, 16, 256, 128), bf16),
            pltpu.VMEM((2, 16, 128, 128), f32),
            pltpu.VMEM((16, 128, 128), f32),
            pltpu.VMEM((256, 128), f32),
            pltpu.VMEM((2, 16, 16, 256), bf16),
            pltpu.VMEM((256, 128), bf16),
            pltpu.VMEM((3, 2, 2, 16, 2, 16, 128), bf16),
            pltpu.VMEM((3, 2, 2, 16, 2, 16, 128), bf16),
            pltpu.VMEM((2, 2, 16, 32, 128), f32),
            pltpu.VMEM((2, 2, 16, 32, 128), f32),
            pltpu.VMEM((2, 8, 32, 128), bf16),
            pltpu.VMEM((2, 16, 32, 128), bf16),
            pltpu.SemaphoreType.DMA((16,)),
            pltpu.SemaphoreType.DMA((3, 2, 2)),
            pltpu.SemaphoreType.DMA((3, 2, 2)),
            pltpu.SemaphoreType.DMA((2, 2)),
            pltpu.SemaphoreType.DMA((2, 2)),
            pltpu.SemaphoreType.DMA((2,)),
            pltpu.SemaphoreType.DMA((2,)),
            pltpu.SemaphoreType.DMA((4,)),
        ],
        compiler_params=pltpu.CompilerParams(
            collective_id=0, has_side_effects=True, vmem_limit_bytes=48 * 1024 * 1024
        ),
    )(
        field.reshape(2, 4096, 128),
        upstream.reshape(2, 4096, 128),
        mode_weights.reshape(16, 2, 256, 128),
        skip_weight,
        channel_bias.reshape(1, 128),
        *[jnp.asarray(table) for table in tables],
    )
    return out.reshape(1, 2, 64, 64, 128), grad.reshape(16, 1, 2, 2, 128, 128)


def solution(mesh):
    in_specs = (
        P("grp", "pen", None, None, None),
        P("grp", "pen", None, None, None),
        P(None, "pen", "grp", None, None, None),
        P(),
        P(),
    )
    out_specs = (P("grp", "pen", None, None, None), P(None, "pen", "grp", None, None, None))
    return jax.shard_map(
        functools.partial(shards, make_tables()), mesh=mesh, in_specs=in_specs, out_specs=out_specs, check_vma=False
    )
```

time: 184 us -> 101 us (0.55); the launches traced: 181 us -> 101 us
  Pallas kernels: 0 us -> 86.7 us
  blocking collectives: 59.8 us -> 0 us
  waiting for transfers between devices: 47.5 us -> 0 us
  matrix products: 44.3 us -> 0 us
  starting transfers between devices: 21.9 us -> 0 us
  local copies, waits for them, and re-layouts: 4.32 us -> 13.2 us
  other arithmetic: 2.31 us -> 0 us
    pallas_call x0 -> x1, Pallas kernels: none -> 86.7 us  [shards(): pl.pallas_call(kernel, out_shape=(jax.ShapeDtypeStruct((2, 4096, 128), bf...]
    all_to_all x4 -> x0, blocking collectives: 59.8 us -> none  [the longest x1 33.8 us: send_pencil(): lax.all_to_all(values, 'pen', split_axis=2, concat_axis=1, tiled=True)]
    all_to_all x2 -> x0, waiting for transfers between devices: 47.5 us -> none  [the longest x1 27 us: send_pencil(): lax.all_to_all(values, 'pen', split_axis=2, concat_axis=1, tiled=True)]
    dot_general x12 -> x0, matrix products: 44.3 us -> none  [the longest x1 17.2 us: from_modes(): jnp.einsum('bxykqc,kqz->bxyzc', planes, depth_back, precision=highest)]
    all_to_all x2 -> x0, starting transfers between devices: 21.9 us -> none  [the longest x1 12.6 us: send_pencil(): lax.all_to_all(values, 'pen', split_axis=2, concat_axis=1, tiled=True)]
    unnamed x16 -> x24, local copies, waits for them, and re-layouts: 0.04 us -> 13.2 us
    transpose x4 -> x0, local copies, waits for them, and re-layouts: 3.91 us -> none  [the longest x2 2.19 us: to_modes(): jnp.einsum('bxykqc,yjqp->bxjkpc', planes, row_table, precision=highest)]
  transfers between devices with their start and end apart: 2 -> 0, of which waited for: 2 -> 0; matrix products, arithmetic and copies ran while one was open for 4% -> 0% of each run, Pallas kernels for 0% -> 0%
where the time goes in v1:
time: 101 us
  Pallas kernels  86.7 us (86%)
  local copies, waits for them, and re-layouts  13.2 us (13%)
    pallas_call x1, Pallas kernels, shards(): pl.pallas_call(kernel, out_shape=(jax.ShapeDtypeStruct((2, 4096, 128), bf...  86.7 us
    unnamed x24, local copies, waits for them, and re-layouts  13.2 us

profile of v1, /device:TPU:1, one launch (start us, length us, event | category | flops | bytes accessed | tf_op | source)
XLA Modules:
  0.0 100.5 jit_solution(3654654142555312937)
XLA Ops:
  0.6 0.0 copy-start
  0.6 1.2 %copy-done = bf16[2,2,512,256]{3,2,1,0:T(8,128)(2,1)S(1)} copy-done((bf16[2,2,512,256]{3,2,1,0:T(8,128)(2,1)S(1)}, bf16[2,2,512,256]{3,2,1,0:T(8,128)(2,1)}, u32[]{:S(2)}) %copy-start) | copy-done | bytes 1048600
  1.9 0.0 copy-start.1
  1.9 1.2 %copy-done.1 = bf16[2,2,512,256]{3,2,1,0:T(8,128)(2,1)S(1)} copy-done((bf16[2,2,512,256]{3,2,1,0:T(8,128)(2,1)S(1)}, bf16[2,2,512,256]{3,2,1,0:T(8,128)(2,1)}, u32[]{:S(2)}) %copy-start.1) | copy-done | bytes 1048600
  3.1 0.0 copy-start.2
  3.1 1.0 %copy-done.2 = bf16[1024,256]{1,0:T(8,128)(2,1)S(1)} copy-done((bf16[1024,256]{1,0:T(8,128)(2,1)S(1)}, bf16[1024,256]{1,0:T(8,128)(2,1)}, u32[]{:S(2)}) %copy-start.2) | copy-done | bytes 524312
  4.1 0.0 copy-start.3
  4.1 0.9 copy-done.3
  5.1 0.0 copy-start.4
  5.1 0.9 copy-done.4
  6.0 0.0 copy-start.5
  6.0 0.9 copy-done.5
  6.9 0.0 copy-start.6
  6.9 0.9 copy-done.6
  7.8 0.0 copy-start.7
  7.8 0.9 copy-done.7
  8.7 0.0 copy-start.8
  8.7 0.8 copy-done.8
  9.5 0.7 copy-done.9
  10.2 86.7 %shard_map.140 = (bf16[2,4096,128]{2,1,0:T(8,128)(2,1)S(1)}, bf16[16,2,256,128]{3,2,1,0:T(8,128)(2,1)}) custom-call(f32[2,4096,128]{2,1,0:T(8,128)} %bitcast.10, bf16[2,4096,128]{2,1,0:T(8,128)(2,1)} %bitcast.12, bf16[16,2,256,128]{3,2,1,0:T(8,128)(2,1)} %bitcast.13, f32[128,128]{1,0:T(8,128)S(1)} %copy-done.8, f32[1,128]{1,0:T(1,128)S(1)} %bitcast.9, ...), custom_call_target="tpu_custom_call" | custom-call | tf_op jit(solution)/shard_map/pallas_call | solution.py:392
  96.9 0.0 copy-start.10
  96.9 1.3 %copy.18 = bf16[1,2,64,64,128]{4,3,2,1,0:T(8,128)(2,1)} copy(bf16[1,2,64,64,128]{4,3,2,1,0:T(8,128)(2,1)S(1)} %bitcast.8) | data formatting | bytes 4194304
  98.2 1.0 %copy-done.10 = bf16[16,2,256,128]{3,2,1,0:T(8,128)(2,1)S(1)} copy-done((bf16[16,2,256,128]{3,2,1,0:T(8,128)(2,1)S(1)}, bf16[16,2,256,128]{3,2,1,0:T(8,128)(2,1)}, u32[]{:S(2)}) %copy-start.10) | copy-done | bytes 2097176
  99.2 1.3 %copy.19 = bf16[16,1,2,2,128,128]{5,4,3,2,1,0:T(8,128)(2,1)} copy(bf16[16,1,2,2,128,128]{5,4,3,2,1,0:T(8,128)(2,1)S(1)} %bitcast.11) | data formatting | bytes 4194304
  (1 shorter events, 0.0 us)
Async XLA Ops:
  0.6 1.2 %copy-start = (bf16[2,2,512,256]{3,2,1,0:T(8,128)(2,1)S(1)}, bf16[2,2,512,256]{3,2,1,0:T(8,128)(2,1)}, u32[]{:S(2)}) copy-start(bf16[2,2,512,256]{3,2,1,0:T(8,128)(2,1)} %constant.19.clone.t4_hbm) | copy-start | bytes 3145732
  1.9 1.2 %copy-start.1 = (bf16[2,2,512,256]{3,2,1,0:T(8,128)(2,1)S(1)}, bf16[2,2,512,256]{3,2,1,0:T(8,128)(2,1)}, u32[]{:S(2)}) copy-start(bf16[2,2,512,256]{3,2,1,0:T(8,128)(2,1)} %constant.18.clone.t3_hbm) | copy-start | bytes 3145732
  3.1 1.0 %copy-start.2 = (bf16[1024,256]{1,0:T(8,128)(2,1)S(1)}, bf16[1024,256]{1,0:T(8,128)(2,1)}, u32[]{:S(2)}) copy-start(bf16[1024,256]{1,0:T(8,128)(2,1)} %constant.20.clone.t5_hbm) | copy-start | bytes 1572868
  4.1 0.9 copy-start.3
  5.1 0.9 copy-start.4
  6.0 0.9 copy-start.5
  6.9 0.9 copy-start.6
  7.8 0.9 copy-start.7
  8.7 0.8 copy-start.8
  9.5 0.7 copy-start.9
  96.9 2.3 %copy-start.10 = (bf16[16,2,256,128]{3,2,1,0:T(8,128)(2,1)S(1)}, bf16[16,2,256,128]{3,2,1,0:T(8,128)(2,1)}, u32[]{:S(2)}) copy-start(bf16[16,2,256,128]{3,2,1,0:T(8,128)(2,1)} %get-tuple-element.5) | copy-start | bytes 6291460

commit v2 on v1

--- a/solution.py
+++ b/solution.py
@@ -122,7 +122,7 @@
     w = g * 2 + x_hi
 
     def ring_peer(i):
-        to = lax.rem(d + i, 16)
+        to = lax.rem(d + 8 + (i // 2) * (2 * lax.rem(i, 2) - 1) + 16, 16)
         return to, (g, x_hi * 16 + to)
 
     def wide_peer(i):
@@ -248,13 +248,14 @@
     for n in range(4):
         quarters[n].wait()
 
-        def depth_loop(m, carry):
+        for m in range(n * 4, n * 4 + 4):
+            here = pl.ds(m * 256, 256)
+            high_0, low_0 = split(field[0, here, :])
+            high_1, low_1 = split(field[1, here, :])
+            both = dot(t1[...], jnp.concatenate([high_0, high_1], axis=1))
+            tile = both[:128] + both[128:] + dot(t1[:128], jnp.concatenate([low_0, low_1], axis=1))
             for e in range(2):
-                values = field[e, pl.ds(pl.multiple_of(m * 256, 256), 256), :]
-                depth_step(e, m, values)
-            return carry
-
-        lax.fori_loop(n * 4, n * 4 + 4, depth_loop, 0)
+                zbuf[e, :, m * 8 : m * 8 + 8, :] = tile[:, e * 128 : e * 128 + 128].reshape(16, 8, 128)
     t2_load.wait()
     for c in range(2):
         for e in range(2):
@@ -268,14 +269,16 @@
     skip_row = jnp.concatenate(split(skip[...]), axis=1)
     skip_both = jnp.concatenate([skip_row, skip_row], axis=0)
 
-    def skip_loop(m, carry):
-        for e in range(2):
-            here = pl.ds(pl.multiple_of(m * 256, 256), 256)
-            both = dot(jnp.concatenate(split(field[e, here, :]), axis=1), skip_both)
-            base[e, here, :] = both[:, :128] + both[:, 128:] + bias[...]
-        return carry
-
-    lax.fori_loop(0, 16, skip_loop, 0)
+    for e in range(2):
+
+        def skip_loop(m, carry):
+            for i in range(8):
+                here = pl.ds(pl.multiple_of(m * 2048 + i * 256, 256), 256)
+                both = dot(jnp.concatenate(split(field[e, here, :]), axis=1), skip_both)
+                base[e, here, :] = both[:, :128] + both[:, 128:] + bias[...]
+            return carry
+
+        lax.fori_loop(0, 2, skip_loop, 0)
 
     t3_load.wait()
     for c in range(2):
@@ -331,16 +334,18 @@
                 ybuf[first : first + 4] = dot_exact(t5[...], values).reshape(4, 128, 128)
 
         def cell_loop(m, carry):
-            values = ybuf[:, pl.ds(pl.multiple_of(m * 8, 8), 8), :].reshape(128, 128)
-            half = jnp.concatenate(split(values), axis=1)
-            both = dot(t6[...], jnp.concatenate([half, half], axis=0))
-            here = pl.ds(pl.multiple_of(m * 256, 256), 256)
-            value, slope = gelu_pair(both[:, :128] + both[:, 128:] + base[e, here, :])
-            out[e, here, :] = value.astype(bf16)
-            depth_step(e, m, slope * up[e, here, :].astype(f32))
-            return carry
-
-        lax.fori_loop(0, 16, cell_loop, 0)
+            for i in range(4):
+                k = m * 4 + i
+                values = ybuf[:, pl.ds(pl.multiple_of(k * 8, 8), 8), :].reshape(128, 128)
+                half = jnp.concatenate(split(values), axis=1)
+                both = dot(t6[...], jnp.concatenate([half, half], axis=0))
+                here = pl.ds(pl.multiple_of(k * 256, 256), 256)
+                value, slope = gelu_pair(both[:, :128] + both[:, 128:] + base[e, here, :])
+                out[e, here, :] = value.astype(bf16)
+                depth_step(e, k, slope * up[e, here, :].astype(f32))
+            return carry
+
+        lax.fori_loop(0, 4, cell_loop, 0)
         store = pltpu.make_async_copy(out.at[e], out_hbm.at[e], store_sem.at[e])
         store.start()
         stores.append(store)
@@ -435,7 +440,7 @@
             pltpu.SemaphoreType.DMA((4,)),
         ],
         compiler_params=pltpu.CompilerParams(
-            collective_id=0, has_side_effects=True, vmem_limit_bytes=48 * 1024 * 1024
+            collective_id=0, has_side_effects=True, vmem_limit_bytes=63 * 1024 * 1024
         ),
     )(
         field.reshape(2, 4096, 128),

time: 101 us -> 78.8 us (0.78)
  Pallas kernels: 86.7 us -> 73.5 us
  local copies, waits for them, and re-layouts: 13.2 us -> 4.55 us
    pallas_call x1, Pallas kernels: 86.7 us -> 73.5 us  [shards(): pl.pallas_call(kernel, out_shape=(jax.ShapeDtypeStruct((2, 4096, 128), bf...]
    unnamed x24 -> x4, local copies, waits for them, and re-layouts: 13.2 us -> 4.55 us
where the time goes in v2:
time: 78.8 us; the launch traced here: 78.7 us
  Pallas kernels  73.5 us (93%)
  local copies, waits for them, and re-layouts  4.55 us (6%)
    pallas_call x1, Pallas kernels, shards(): pl.pallas_call(kernel, out_shape=(jax.ShapeDtypeStruct((2, 4096, 128), bf...  73.5 us
    unnamed x4, local copies, waits for them, and re-layouts  4.55 us

profile of v2, /device:TPU:1, one launch (start us, length us, event | category | flops | bytes accessed | tf_op | source)
XLA Modules:
  0.0 78.7 jit_solution(1061272831902071745)
XLA Ops:
  0.6 73.5 %shard_map.140 = (bf16[2,4096,128]{2,1,0:T(8,128)(2,1)}, bf16[16,2,256,128]{3,2,1,0:T(8,128)(2,1)}) custom-call(f32[2,4096,128]{2,1,0:T(8,128)} %bitcast.8, bf16[2,4096,128]{2,1,0:T(8,128)(2,1)} %bitcast.11, bf16[16,2,256,128]{3,2,1,0:T(8,128)(2,1)} %bitcast.12, f32[128,128]{1,0:T(8,128)} %skip_hbm.1, f32[1,128]{1,0:T(1,128)} %bitcast.13, ...), custom_call_target="tpu_custom_call" | custom-call | tf_op jit(solution)/shard_map/pallas_call | solution.py:397
  74.2 0.0 copy-start
  74.2 3.2 %copy.18 = bf16[1,2,64,64,128]{4,3,2,1,0:T(8,128)(2,1)} copy(bf16[1,2,64,64,128]{4,3,2,1,0:T(8,128)(2,1)} %bitcast.10) | data formatting | bytes 4194304
  77.4 0.0 copy-done
  77.4 1.3 %copy.19 = bf16[16,1,2,2,128,128]{5,4,3,2,1,0:T(8,128)(2,1)} copy(bf16[16,1,2,2,128,128]{5,4,3,2,1,0:T(8,128)(2,1)S(1)} %bitcast.9) | data formatting | bytes 4194304
Async XLA Ops:
  74.2 3.2 %copy-start = (bf16[16,2,256,128]{3,2,1,0:T(8,128)(2,1)S(1)}, bf16[16,2,256,128]{3,2,1,0:T(8,128)(2,1)}, u32[]{:S(2)}) copy-start(bf16[16,2,256,128]{3,2,1,0:T(8,128)(2,1)} %get-tuple-element.5) | copy-start | bytes 6291460

commit v3 on v2

--- a/solution.py
+++ b/solution.py
@@ -83,27 +83,9 @@
     return both[:rows] + both[rows:]
 
 
-SCALED = (
-    0.11283793162135076,
-    0.11283476245314182,
-    0.10392192770562217,
-    0.0842669599289443,
-    0.07073040277585074,
-    -0.002833797179664962,
-    0.08457735964663142,
-    -0.09147177273287684,
-    0.025136288482206462,
-)
-
-
 def gelu_pair(v):
-    bell = jnp.exp(-0.5 * (v * v))
-    t = 1.0 / (1.0 + 0.282842712474619 * jnp.abs(v))
-    series = jnp.full_like(t, SCALED[-1] * 1.0)
-    for coefficient in SCALED[-2::-1]:
-        series = series * t + coefficient
-    tail = bell * (t * series)
-    phi = jnp.where(v >= 0, 1.0 - tail, tail)
+    phi = 0.5 + 0.5 * lax.erf(v * math.sqrt(0.5))
+    bell = jnp.exp2((v * v) * (-0.5 * math.log2(math.e)))
     return v * phi, phi + v * (bell * (1.0 / math.sqrt(2.0 * math.pi)))
 
 
@@ -112,14 +94,15 @@
     out_hbm, grad_hbm,
     field, up, weight, skip, bias, t1, t2, t3, t4, t5, t6, gather, scatter,
     base, out, grad, zbuf, ybuf, rows, pairs, mixed,
-    ring_send, ring_recv, wide_send, wide_recv, back_send, back_recv,
-    load_sem, ring_ssem, ring_rsem, wide_ssem, wide_rsem, back_ssem, back_rsem, store_sem,
+    first_send, first_recv, ring_send, ring_recv, wide_send, wide_recv, back_send, back_recv,
+    load_sem, first_ssem, first_rsem, ring_ssem, ring_rsem, wide_ssem, wide_rsem, back_ssem, back_rsem, store_sem,
 ):
     g = lax.axis_index("grp")
     p = lax.axis_index("pen")
     x_hi = p // 16
     d = lax.rem(p, 16)
     w = g * 2 + x_hi
+    half_g = g // 4
 
     def ring_peer(i):
         to = lax.rem(d + 8 + (i // 2) * (2 * lax.rem(i, 2) - 1) + 16, 16)
@@ -153,6 +136,128 @@
     t2_load = load(t2_hbm, t2)
     skip_load = load(skip_hbm, skip)
     bias_load = load(bias_hbm, bias)
+
+    def ring_start(source, target, ssem, rsem):
+        pltpu.make_async_copy(source.at[d], target.at[d], rsem).start()
+
+        def send(i, carry):
+            to, device = ring_peer(i)
+            pltpu.make_async_remote_copy(
+                src_ref=source.at[to],
+                dst_ref=target.at[d],
+                send_sem=ssem,
+                recv_sem=rsem,
+                device_id=device,
+                device_id_type=MESH,
+            ).start()
+            return carry
+
+        lax.fori_loop(1, 16, send, 0)
+
+    def first_sent(c, q):
+        drain(first_send.at[c, q, pl.ds(0, 15)], first_ssem.at[c, q])
+
+    def plane_sent(n, e, c):
+        drain(ring_send.at[n, e, c, pl.ds(0, 15)], ring_ssem.at[n, e, c])
+
+    def first_start(c, q):
+        ring_start(first_send.at[c, q], first_recv.at[c, q], first_ssem.at[c, q], first_rsem.at[c, q])
+
+    def plane_start(n, e, c):
+        ring_start(ring_send.at[n, e, c], ring_recv.at[n, e, c], ring_ssem.at[n, e, c], ring_rsem.at[n, e, c])
+
+    def wide_start(n, c, q):
+        source, target = wide_send.at[n, c, q], wide_recv.at[n, c]
+        slot = x_hi * 8 + g
+        mine = lax.rem(w, 8)
+
+        def send(i, carry):
+            to = lax.rem(mine + i, 8)
+            pltpu.make_async_remote_copy(
+                src_ref=source.at[to],
+                dst_ref=target.at[slot],
+                send_sem=wide_ssem.at[n, c, q],
+                recv_sem=wide_rsem.at[n, c],
+                device_id=(q * 4 + to // 2, lax.rem(to, 2) * 16 + d),
+                device_id_type=MESH,
+            ).start()
+            return carry
+
+        lax.fori_loop(1, 8, send, 0)
+
+        @pl.when(half_g == q)
+        def _():
+            pltpu.make_async_copy(source.at[mine], target.at[slot], wide_rsem.at[n, c]).start()
+
+        @pl.when(half_g != q)
+        def _():
+            send(0, 0)
+
+    def wide_drain(n, c, q):
+        sent = wide_send.at[n, c, q]
+
+        @pl.when(half_g == q)
+        def _():
+            drain(sent.at[pl.ds(0, 7)], wide_ssem.at[n, c, q])
+
+        @pl.when(half_g != q)
+        def _():
+            drain(sent, wide_ssem.at[n, c, q])
+
+    def back_start(c):
+        source, target = back_send.at[c], back_recv.at[c]
+        slot = (g // 4) * 8 + x_hi * 4 + lax.rem(g, 4)
+        pltpu.make_async_copy(source.at[g], target.at[slot], back_rsem.at[c, half_g]).start()
+
+        def send(i, carry):
+            to, device = wide_peer(i)
+            pltpu.make_async_remote_copy(
+                src_ref=source.at[to // 2],
+                dst_ref=target.at[slot],
+                send_sem=back_ssem.at[c],
+                recv_sem=back_rsem.at[c, half_g],
+                device_id=device,
+                device_id_type=MESH,
+            ).start()
+            return carry
+
+        lax.fori_loop(1, 16, send, 0)
+
+    def drain(buffer, semaphore):
+        pltpu.make_async_copy(buffer, buffer, semaphore).wait()
+
+    def depth_step(e, m, values):
+        tile = dot_split(t1[...], values).reshape(16, 8, 128)
+        zbuf[e, :, pl.ds(pl.multiple_of(m * 8, 8), 8), :] = tile
+
+    def row_step(e, c, q):
+        tiles = []
+        for half in range(2):
+            first = c * 8 + q * 4 + half * 2
+            values = zbuf[e, first : first + 2].reshape(256, 128)
+            tiles.append(dot_split(t2[...], values).reshape(16, 8, 128))
+        return jnp.concatenate(tiles, axis=1).astype(bf16)
+
+    def plane_step(n, c, q, plane_0, plane_1):
+        total = dot_exact(t3[0], plane_0.reshape(256, 128)) + dot_exact(t3[1], plane_1.reshape(256, 128))
+        wide_send[n, c, q] = total.reshape(8, 32, 128)
+
+    def collect(n, c):
+        summed = (wide_recv[n, c, 0:8] + wide_recv[n, c, 8:16]).reshape(256, 128)
+        rows[...] = dot(gather[...], jnp.concatenate(split(summed), axis=0))
+
+    t1_load.wait()
+    for n in range(4):
+        quarters[n].wait()
+
+        for m in range(n * 4, n * 4 + 4):
+            here = pl.ds(m * 256, 256)
+            high_0, low_0 = split(field[0, here, :])
+            high_1, low_1 = split(field[1, here, :])
+            both = dot(t1[...], jnp.concatenate([high_0, high_1], axis=1))
+            tile = both[:128] + both[128:] + dot(t1[:128], jnp.concatenate([low_0, low_1], axis=1))
+            for e in range(2):
+                zbuf[e, :, m * 8 : m * 8 + 8, :] = tile[:, e * 128 : e * 128 + 128].reshape(16, 8, 128)
     t3_load = load(t3_hbm.at[x_hi], t3)
     gather_load = load(gather_hbm, gather)
     weight_load = load(weight_hbm, weight)
@@ -161,108 +266,15 @@
     t5_load = load(t5_hbm, t5)
     t6_load = load(t6_hbm, t6)
     up_load = load(up_hbm, up)
-
-    def ring_start(n, e, c):
-        source, target = ring_send.at[n, e, c], ring_recv.at[n, e, c]
-        pltpu.make_async_copy(source.at[d], target.at[d], ring_rsem.at[n, e, c]).start()
-
-        def send(i, carry):
-            to, device = ring_peer(i)
-            pltpu.make_async_remote_copy(
-                src_ref=source.at[to],
-                dst_ref=target.at[d],
-                send_sem=ring_ssem.at[n, e, c],
-                recv_sem=ring_rsem.at[n, e, c],
-                device_id=device,
-                device_id_type=MESH,
-            ).start()
-            return carry
-
-        lax.fori_loop(1, 16, send, 0)
-
-    def wide_start(n, c):
-        source, target = wide_send.at[n, c], wide_recv.at[n, c]
-        slot = x_hi * 8 + g
-        pltpu.make_async_copy(source.at[w], target.at[slot], wide_rsem.at[n, c]).start()
-
-        def send(i, carry):
-            to, device = wide_peer(i)
-            pltpu.make_async_remote_copy(
-                src_ref=source.at[to],
-                dst_ref=target.at[slot],
-                send_sem=wide_ssem.at[n, c],
-                recv_sem=wide_rsem.at[n, c],
-                device_id=device,
-                device_id_type=MESH,
-            ).start()
-            return carry
-
-        lax.fori_loop(1, 16, send, 0)
-
-    def back_start(c):
-        source, target = back_send.at[c], back_recv.at[c]
-        slot = (g // 4) * 8 + x_hi * 4 + lax.rem(g, 4)
-        pltpu.make_async_copy(source.at[g], target.at[slot], back_rsem.at[c]).start()
-
-        def send(i, carry):
-            to, device = wide_peer(i)
-            pltpu.make_async_remote_copy(
-                src_ref=source.at[to // 2],
-                dst_ref=target.at[slot],
-                send_sem=back_ssem.at[c],
-                recv_sem=back_rsem.at[c],
-                device_id=device,
-                device_id_type=MESH,
-            ).start()
-            return carry
-
-        lax.fori_loop(1, 16, send, 0)
-
-    def drain(buffer, semaphore):
-        pltpu.make_async_copy(buffer, buffer, semaphore).wait()
-
-    def depth_step(e, m, values):
-        tile = dot_split(t1[...], values).reshape(16, 8, 128)
-        zbuf[e, :, pl.ds(pl.multiple_of(m * 8, 8), 8), :] = tile
-
-    def row_step(n, e, c):
+    t2_load.wait()
+    for c in range(2):
         for q in range(2):
-            tiles = []
-            for half in range(2):
-                first = c * 8 + q * 4 + half * 2
-                values = zbuf[e, first : first + 2].reshape(256, 128)
-                tiles.append(dot_split(t2[...], values).reshape(16, 8, 128))
-            ring_send[n, e, c, :, q] = jnp.concatenate(tiles, axis=1).astype(bf16)
-
-    def plane_step(n, c):
-        for q in range(2):
-            total = dot_exact(t3[0], ring_recv[n, 0, c, :, q].reshape(256, 128))
-            total += dot_exact(t3[1], ring_recv[n, 1, c, :, q].reshape(256, 128))
-            wide_send[n // 2, c, q * 8 : q * 8 + 8] = total.reshape(8, 32, 128)
-
-    def collect(n, c):
-        summed = (wide_recv[n, c, 0:8] + wide_recv[n, c, 8:16]).reshape(256, 128)
-        rows[...] = dot(gather[...], jnp.concatenate(split(summed), axis=0))
-
-    t1_load.wait()
-    for n in range(4):
-        quarters[n].wait()
-
-        for m in range(n * 4, n * 4 + 4):
-            here = pl.ds(m * 256, 256)
-            high_0, low_0 = split(field[0, here, :])
-            high_1, low_1 = split(field[1, here, :])
-            both = dot(t1[...], jnp.concatenate([high_0, high_1], axis=1))
-            tile = both[:128] + both[128:] + dot(t1[:128], jnp.concatenate([low_0, low_1], axis=1))
             for e in range(2):
-                zbuf[e, :, m * 8 : m * 8 + 8, :] = tile[:, e * 128 : e * 128 + 128].reshape(16, 8, 128)
-    t2_load.wait()
-    for c in range(2):
-        for e in range(2):
-            row_step(0, e, c)
-            if c == 0 and e == 0:
+                first_send[c, q, :, e] = row_step(e, c, q)
+            if c + q == 0:
                 pl.semaphore_wait(barrier, 30)
-            ring_start(0, e, c)
+            if c == 0:
+                first_start(c, q)
 
     skip_load.wait()
     bias_load.wait()
@@ -279,13 +291,15 @@
             return carry
 
         lax.fori_loop(0, 2, skip_loop, 0)
+        first_sent(0, e)
+        first_start(1, e)
 
     t3_load.wait()
     for c in range(2):
-        for e in range(2):
-            drain(ring_recv.at[0, e, c], ring_rsem.at[0, e, c])
-        plane_step(0, c)
-        wide_start(0, c)
+        for q in range(2):
+            drain(first_recv.at[c, q], first_rsem.at[c, q])
+            plane_step(0, c, q, first_recv[c, q, :, 0], first_recv[c, q, :, 1])
+            wide_start(0, c, q)
 
     gather_load.wait()
     weight_load.wait()
@@ -312,14 +326,16 @@
 
     t4_load.wait()
     for c in range(2):
-        drain(back_recv.at[c], back_rsem.at[c])
         for q in range(2):
+            drain(back_recv.at[c, pl.ds(q * 8, 8)], back_rsem.at[c, q])
             values = back_recv[c, q * 8 : q * 8 + 8].reshape(256, 128)
             for e in range(2):
-                ring_send[1, e, c, :, q] = dot_exact(t4[e], values).reshape(16, 16, 128).astype(bf16)
-        ring_start(1, 0, c)
-    ring_start(1, 1, 0)
-    ring_start(1, 1, 1)
+                ring_send[0, e, c, :, q] = dot_exact(t4[e], values).reshape(16, 16, 128).astype(bf16)
+        plane_start(0, 0, c)
+        if c == 0:
+            plane_start(0, 1, 0)
+    plane_sent(0, 0, 1)
+    plane_start(0, 1, 1)
 
     t5_load.wait()
     t6_load.wait()
@@ -327,15 +343,15 @@
     stores = []
     for e in range(2):
         for c in range(2):
-            drain(ring_recv.at[1, e, c], ring_rsem.at[1, e, c])
+            drain(ring_recv.at[0, e, c], ring_rsem.at[0, e, c])
             for q in range(2):
                 first = c * 8 + q * 4
-                values = ring_recv[1, e, c, :, q].reshape(256, 128)
+                values = ring_recv[0, e, c, :, q].reshape(256, 128)
                 ybuf[first : first + 4] = dot_exact(t5[...], values).reshape(4, 128, 128)
 
         def cell_loop(m, carry):
-            for i in range(4):
-                k = m * 4 + i
+            for i in range(8):
+                k = m * 8 + i
                 values = ybuf[:, pl.ds(pl.multiple_of(k * 8, 8), 8), :].reshape(128, 128)
                 half = jnp.concatenate(split(values), axis=1)
                 both = dot(t6[...], jnp.concatenate([half, half], axis=0))
@@ -345,19 +361,23 @@
                 depth_step(e, k, slope * up[e, here, :].astype(f32))
             return carry
 
-        lax.fori_loop(0, 4, cell_loop, 0)
+        lax.fori_loop(0, 2, cell_loop, 0)
         store = pltpu.make_async_copy(out.at[e], out_hbm.at[e], store_sem.at[e])
         store.start()
         stores.append(store)
         for c in range(2):
-            row_step(2, e, c)
-            ring_start(2, e, c)
+            for q in range(2):
+                ring_send[1, e, c, :, q] = row_step(e, c, q)
+            if e == 1:
+                plane_sent(1, 0, c)
+            plane_start(1, e, c)
 
     for c in range(2):
         for e in range(2):
-            drain(ring_recv.at[2, e, c], ring_rsem.at[2, e, c])
-        plane_step(2, c)
-        wide_start(1, c)
+            drain(ring_recv.at[1, e, c], ring_rsem.at[1, e, c])
+        for q in range(2):
+            plane_step(1, c, q, ring_recv[1, 0, c, :, q], ring_recv[1, 1, c, :, q])
+            wide_start(1, c, q)
 
     for c in range(2):
         drain(wide_recv.at[1, c], wide_rsem.at[1, c])
@@ -379,13 +399,15 @@
         store.start()
         stores.append(store)
 
-    for n in range(3):
-        for e in range(2):
-            for c in range(2):
-                drain(ring_send.at[n, e, c, pl.ds(0, 15)], ring_ssem.at[n, e, c])
     for n in range(2):
         for c in range(2):
-            drain(wide_send.at[n, c, pl.ds(0, 15)], wide_ssem.at[n, c])
+            for q in range(2):
+                wide_drain(n, c, q)
+    for e, c in ((0, 0), (1, 0), (1, 1)):
+        plane_sent(0, e, c)
+    for c in range(2):
+        plane_sent(1, 1, c)
+        first_sent(1, c)
     for c in range(2):
         drain(back_recv.at[c, pl.ds(0, 15)], back_ssem.at[c])
     for store in stores:
@@ -424,19 +446,23 @@
             pltpu.VMEM((256, 128), f32),
             pltpu.VMEM((2, 16, 16, 256), bf16),
             pltpu.VMEM((256, 128), bf16),
-            pltpu.VMEM((3, 2, 2, 16, 2, 16, 128), bf16),
-            pltpu.VMEM((3, 2, 2, 16, 2, 16, 128), bf16),
-            pltpu.VMEM((2, 2, 16, 32, 128), f32),
+            pltpu.VMEM((2, 2, 16, 2, 16, 128), bf16),
+            pltpu.VMEM((2, 2, 16, 2, 16, 128), bf16),
+            pltpu.VMEM((2, 2, 2, 16, 2, 16, 128), bf16),
+            pltpu.VMEM((2, 2, 2, 16, 2, 16, 128), bf16),
+            pltpu.VMEM((2, 2, 2, 8, 32, 128), f32),
             pltpu.VMEM((2, 2, 16, 32, 128), f32),
             pltpu.VMEM((2, 8, 32, 128), bf16),
             pltpu.VMEM((2, 16, 32, 128), bf16),
             pltpu.SemaphoreType.DMA((16,)),
-            pltpu.SemaphoreType.DMA((3, 2, 2)),
-            pltpu.SemaphoreType.DMA((3, 2, 2)),
             pltpu.SemaphoreType.DMA((2, 2)),
             pltpu.SemaphoreType.DMA((2, 2)),
+            pltpu.SemaphoreType.DMA((2, 2, 2)),
+            pltpu.SemaphoreType.DMA((2, 2, 2)),
+            pltpu.SemaphoreType.DMA((2, 2, 2)),
+            pltpu.SemaphoreType.DMA((2, 2)),
             pltpu.SemaphoreType.DMA((2,)),
-            pltpu.SemaphoreType.DMA((2,)),
+            pltpu.SemaphoreType.DMA((2, 2)),
             pltpu.SemaphoreType.DMA((4,)),
         ],
         compiler_params=pltpu.CompilerParams(

time: 78.8 us -> 75.5 us (0.958)
  Pallas kernels: 73.5 us -> 70.2 us
    pallas_call x1, Pallas kernels: 73.5 us -> 70.2 us  [shards(): pl.pallas_call(kernel, out_shape=(jax.ShapeDtypeStruct((2, 4096, 128), bf...]
where the time goes in v3:
time: 75.5 us; the launch traced here: 75.4 us
  Pallas kernels  70.2 us (93%)
  local copies, waits for them, and re-layouts  4.55 us (6%)
    pallas_call x1, Pallas kernels, shards(): pl.pallas_call(kernel, out_shape=(jax.ShapeDtypeStruct((2, 4096, 128), bf...  70.2 us
    unnamed x4, local copies, waits for them, and re-layouts  4.55 us

profile of v3, /device:TPU:1, one launch (start us, length us, event | category | flops | bytes accessed | tf_op | source)
XLA Modules:
  0.0 75.4 jit_solution(2075441966059196200)
XLA Ops:
  0.6 70.2 %shard_map.140 = (bf16[2,4096,128]{2,1,0:T(8,128)(2,1)}, bf16[16,2,256,128]{3,2,1,0:T(8,128)(2,1)}) custom-call(f32[2,4096,128]{2,1,0:T(8,128)} %bitcast.8, bf16[2,4096,128]{2,1,0:T(8,128)(2,1)} %bitcast.11, bf16[16,2,256,128]{3,2,1,0:T(8,128)(2,1)} %bitcast.12, f32[128,128]{1,0:T(8,128)} %skip_hbm.1, f32[1,128]{1,0:T(1,128)} %bitcast.13, ...), custom_call_target="tpu_custom_call" | custom-call | tf_op jit(solution)/shard_map/pallas_call | solution.py:419
  70.9 0.0 copy-start
  70.9 3.2 %copy.18 = bf16[1,2,64,64,128]{4,3,2,1,0:T(8,128)(2,1)} copy(bf16[1,2,64,64,128]{4,3,2,1,0:T(8,128)(2,1)} %bitcast.10) | data formatting | bytes 4194304
  74.1 0.0 copy-done
  74.1 1.3 %copy.19 = bf16[16,1,2,2,128,128]{5,4,3,2,1,0:T(8,128)(2,1)} copy(bf16[16,1,2,2,128,128]{5,4,3,2,1,0:T(8,128)(2,1)S(1)} %bitcast.9) | data formatting | bytes 4194304
Async XLA Ops:
  70.9 3.2 %copy-start = (bf16[16,2,256,128]{3,2,1,0:T(8,128)(2,1)S(1)}, bf16[16,2,256,128]{3,2,1,0:T(8,128)(2,1)}, u32[]{:S(2)}) copy-start(bf16[16,2,256,128]{3,2,1,0:T(8,128)(2,1)} %get-tuple-element.5) | copy-start | bytes 6291460

commit v4 on v3

--- a/solution.py
+++ b/solution.py
@@ -114,13 +114,6 @@
 
     barrier = pltpu.get_barrier_semaphore()
 
-    def greet(i, carry):
-        for peer in (ring_peer, wide_peer):
-            pl.semaphore_signal(barrier, inc=1, device_id=peer(i)[1], device_id_type=MESH)
-        return carry
-
-    lax.fori_loop(1, 16, greet, 0)
-
     loads = []
 
     def load(source, target):
@@ -130,10 +123,16 @@
         return copy
 
     t1_load = load(t1_hbm, t1)
-    quarters = [
-        load(field_hbm.at[:, pl.ds(n * 1024, 1024), :], field.at[:, pl.ds(n * 1024, 1024), :]) for n in range(4)
+    pieces = [
+        load(field_hbm.at[:, pl.ds(n * 512, 512), :], field.at[:, pl.ds(n * 512, 512), :]) for n in range(8)
     ]
     t2_load = load(t2_hbm, t2)
+    def greet(i, carry):
+        for peer in (ring_peer, wide_peer):
+            pl.semaphore_signal(barrier, inc=1, device_id=peer(i)[1], device_id_type=MESH)
+        return carry
+
+    lax.fori_loop(1, 16, greet, 0)
     skip_load = load(skip_hbm, skip)
     bias_load = load(bias_hbm, bias)
 
@@ -247,10 +246,10 @@
         rows[...] = dot(gather[...], jnp.concatenate(split(summed), axis=0))
 
     t1_load.wait()
-    for n in range(4):
-        quarters[n].wait()
-
-        for m in range(n * 4, n * 4 + 4):
+    for n in range(8):
+        pieces[n].wait()
+
+        for m in range(n * 2, n * 2 + 2):
             here = pl.ds(m * 256, 256)
             high_0, low_0 = split(field[0, here, :])
             high_1, low_1 = split(field[1, here, :])
@@ -309,8 +308,8 @@
         collect(0, c)
 
         def mix_loop(m, carry):
-            for i in range(4):
-                k = m * 4 + i
+            for i in range(8):
+                k = m * 8 + i
                 real = rows[pl.ds(pl.multiple_of(k * 16, 16), 8), :]
                 imag = rows[pl.ds(pl.multiple_of(k * 16 + 8, 8), 8), :]
                 upper = jnp.concatenate([real, -imag], axis=1)
@@ -320,7 +319,7 @@
                 mixed[pl.ds(pl.multiple_of(k * 16, 16), 16), :] = dot(paired, weight[k, c]).astype(bf16)
             return carry
 
-        lax.fori_loop(0, 4, mix_loop, 0)
+        lax.fori_loop(0, 2, mix_loop, 0)
         back_send[c] = dot(scatter[...], mixed[...]).astype(bf16).reshape(8, 32, 128)
         back_start(c)
 
@@ -332,8 +331,7 @@
             for e in range(2):
                 ring_send[0, e, c, :, q] = dot_exact(t4[e], values).reshape(16, 16, 128).astype(bf16)
         plane_start(0, 0, c)
-        if c == 0:
-            plane_start(0, 1, 0)
+    plane_start(0, 1, 0)
     plane_sent(0, 0, 1)
     plane_start(0, 1, 1)
 
@@ -368,8 +366,11 @@
         for c in range(2):
             for q in range(2):
                 ring_send[1, e, c, :, q] = row_step(e, c, q)
-            if e == 1:
-                plane_sent(1, 0, c)
+            if e == 1 and c == 0:
+                plane_sent(1, 0, 0)
+            if e == 1 and c == 1:
+                plane_sent(1, 0, 1)
+                plane_sent(1, 1, 0)
             plane_start(1, e, c)
 
     for c in range(2):
@@ -384,20 +385,17 @@
         collect(1, c)
         scale = jnp.where(g == 0, 1.0, 2.0).astype(f32) if c == 0 else f32(2.0)
 
-        def grad_loop(m, carry):
-            for i in range(4):
-                k = m * 4 + i
-                cotangent = (rows[pl.ds(pl.multiple_of(k * 16, 16), 16), :] * scale).astype(bf16)
+        for half in range(2):
+            for k in range(half * 8, half * 8 + 8):
+                cotangent = (rows[k * 16 : k * 16 + 16, :] * scale).astype(bf16)
                 product = lax.dot_general(
                     pairs[c, k], cotangent, (((0,), (0,)), ((), ())), preferred_element_type=f32
                 )
                 grad[c, k] = product.astype(bf16)
-            return carry
-
-        lax.fori_loop(0, 4, grad_loop, 0)
-        store = pltpu.make_async_copy(grad.at[c], grad_hbm.at[:, c], store_sem.at[2 + c])
-        store.start()
-        stores.append(store)
+            part = pl.ds(half * 8, 8)
+            store = pltpu.make_async_copy(grad.at[c, part], grad_hbm.at[part, c], store_sem.at[2 + 2 * c + half])
+            store.start()
+            stores.append(store)
 
     for n in range(2):
         for c in range(2):
@@ -406,8 +404,8 @@
     for e, c in ((0, 0), (1, 0), (1, 1)):
         plane_sent(0, e, c)
     for c in range(2):
-        plane_sent(1, 1, c)
         first_sent(1, c)
+    plane_sent(1, 1, 1)
     for c in range(2):
         drain(back_recv.at[c, pl.ds(0, 15)], back_ssem.at[c])
     for store in stores:
@@ -454,7 +452,7 @@
             pltpu.VMEM((2, 2, 16, 32, 128), f32),
             pltpu.VMEM((2, 8, 32, 128), bf16),
             pltpu.VMEM((2, 16, 32, 128), bf16),
-            pltpu.SemaphoreType.DMA((16,)),
+            pltpu.SemaphoreType.DMA((20,)),
             pltpu.SemaphoreType.DMA((2, 2)),
             pltpu.SemaphoreType.DMA((2, 2)),
             pltpu.SemaphoreType.DMA((2, 2, 2)),
@@ -463,7 +461,7 @@
             pltpu.SemaphoreType.DMA((2, 2)),
             pltpu.SemaphoreType.DMA((2,)),
             pltpu.SemaphoreType.DMA((2, 2)),
-            pltpu.SemaphoreType.DMA((4,)),
+            pltpu.SemaphoreType.DMA((6,)),
         ],
         compiler_params=pltpu.CompilerParams(
             collective_id=0, has_side_effects=True, vmem_limit_bytes=63 * 1024 * 1024

time: 75.5 us -> 73.2 us (0.970)
  Pallas kernels: 70.2 us -> 67.9 us
    pallas_call x1, Pallas kernels: 70.2 us -> 67.9 us  [shards(): pl.pallas_call(kernel, out_shape=(jax.ShapeDtypeStruct((2, 4096, 128), bf...]
where the time goes in v4:
time: 73.2 us; the launch traced here: 73.1 us
  Pallas kernels  67.9 us (93%)
  local copies, waits for them, and re-layouts  4.55 us (6%)
    pallas_call x1, Pallas kernels, shards(): pl.pallas_call(kernel, out_shape=(jax.ShapeDtypeStruct((2, 4096, 128), bf...  67.9 us
    unnamed x4, local copies, waits for them, and re-layouts  4.55 us

profile of v4, /device:TPU:1, one launch (start us, length us, event | category | flops | bytes accessed | tf_op | source)
XLA Modules:
  0.0 73.1 jit_solution(12756882586630273264)
XLA Ops:
  0.6 67.9 %shard_map.140 = (bf16[2,4096,128]{2,1,0:T(8,128)(2,1)}, bf16[16,2,256,128]{3,2,1,0:T(8,128)(2,1)}) custom-call(f32[2,4096,128]{2,1,0:T(8,128)} %bitcast.8, bf16[2,4096,128]{2,1,0:T(8,128)(2,1)} %bitcast.11, bf16[16,2,256,128]{3,2,1,0:T(8,128)(2,1)} %bitcast.12, f32[128,128]{1,0:T(8,128)} %skip_hbm.1, f32[1,128]{1,0:T(1,128)} %bitcast.13, ...), custom_call_target="tpu_custom_call" | custom-call | tf_op jit(solution)/shard_map/pallas_call | solution.py:417
  68.6 0.0 copy-start
  68.6 3.2 %copy.18 = bf16[1,2,64,64,128]{4,3,2,1,0:T(8,128)(2,1)} copy(bf16[1,2,64,64,128]{4,3,2,1,0:T(8,128)(2,1)} %bitcast.10) | data formatting | bytes 4194304
  71.8 0.0 copy-done
  71.8 1.3 %copy.19 = bf16[16,1,2,2,128,128]{5,4,3,2,1,0:T(8,128)(2,1)} copy(bf16[16,1,2,2,128,128]{5,4,3,2,1,0:T(8,128)(2,1)S(1)} %bitcast.9) | data formatting | bytes 4194304
Async XLA Ops:
  68.6 3.2 %copy-start = (bf16[16,2,256,128]{3,2,1,0:T(8,128)(2,1)S(1)}, bf16[16,2,256,128]{3,2,1,0:T(8,128)(2,1)}, u32[]{:S(2)}) copy-start(bf16[16,2,256,128]{3,2,1,0:T(8,128)(2,1)} %get-tuple-element.5) | copy-start | bytes 6291460

commit v5 on v4

--- a/solution.py
+++ b/solution.py
@@ -348,8 +348,8 @@
                 ybuf[first : first + 4] = dot_exact(t5[...], values).reshape(4, 128, 128)
 
         def cell_loop(m, carry):
-            for i in range(8):
-                k = m * 8 + i
+            for i in range(16):
+                k = m * 16 + i
                 values = ybuf[:, pl.ds(pl.multiple_of(k * 8, 8), 8), :].reshape(128, 128)
                 half = jnp.concatenate(split(values), axis=1)
                 both = dot(t6[...], jnp.concatenate([half, half], axis=0))
@@ -359,7 +359,7 @@
                 depth_step(e, k, slope * up[e, here, :].astype(f32))
             return carry
 
-        lax.fori_loop(0, 2, cell_loop, 0)
+        lax.fori_loop(0, 1, cell_loop, 0)
         store = pltpu.make_async_copy(out.at[e], out_hbm.at[e], store_sem.at[e])
         store.start()
         stores.append(store)

time: 73.2 us -> 73.1 us (level)
  no operation moved by 1% of the time
where the time goes in v5:
time: 73.1 us; the launch traced here: 73 us
  Pallas kernels  67.8 us (93%)
  local copies, waits for them, and re-layouts  4.55 us (6%)
    pallas_call x1, Pallas kernels, shards(): pl.pallas_call(kernel, out_shape=(jax.ShapeDtypeStruct((2, 4096, 128), bf...  67.8 us
    unnamed x4, local copies, waits for them, and re-layouts  4.55 us

profile of v5, /device:TPU:1, one launch (start us, length us, event | category | flops | bytes accessed | tf_op | source)
XLA Modules:
  0.0 73.0 jit_solution(4550269283446781320)
XLA Ops:
  0.6 67.8 %shard_map.140 = (bf16[2,4096,128]{2,1,0:T(8,128)(2,1)}, bf16[16,2,256,128]{3,2,1,0:T(8,128)(2,1)}) custom-call(f32[2,4096,128]{2,1,0:T(8,128)} %bitcast.8, bf16[2,4096,128]{2,1,0:T(8,128)(2,1)} %bitcast.11, bf16[16,2,256,128]{3,2,1,0:T(8,128)(2,1)} %bitcast.12, f32[128,128]{1,0:T(8,128)} %skip_hbm.1, f32[1,128]{1,0:T(1,128)} %bitcast.13, ...), custom_call_target="tpu_custom_call" | custom-call | tf_op jit(solution)/shard_map/pallas_call | solution.py:417
  68.5 0.0 copy-start
  68.5 3.2 %copy.18 = bf16[1,2,64,64,128]{4,3,2,1,0:T(8,128)(2,1)} copy(bf16[1,2,64,64,128]{4,3,2,1,0:T(8,128)(2,1)} %bitcast.10) | data formatting | bytes 4194304
  71.7 0.0 copy-done
  71.7 1.3 %copy.19 = bf16[16,1,2,2,128,128]{5,4,3,2,1,0:T(8,128)(2,1)} copy(bf16[16,1,2,2,128,128]{5,4,3,2,1,0:T(8,128)(2,1)S(1)} %bitcast.9) | data formatting | bytes 4194304
Async XLA Ops:
  68.5 3.2 %copy-start = (bf16[16,2,256,128]{3,2,1,0:T(8,128)(2,1)S(1)}, bf16[16,2,256,128]{3,2,1,0:T(8,128)(2,1)}, u32[]{:S(2)}) copy-start(bf16[16,2,256,128]{3,2,1,0:T(8,128)(2,1)} %get-tuple-element.5) | copy-start | bytes 6291460
